TPU v7x, 128 devices: a whole 4x4x4 slice. The times are simulated.
128 devices in a mesh: shard: 4 (over y_lo, core), replica: 32 (over y_hi, z, x).
Axes of the slice: x: 4, y: 4 (y_hi: 2, y_lo: 2; y = y_hi * 2 + y_lo), z: 4, core: 2. Of those that a mesh axis runs over, the one named last changes fastest.
Arguments:
- tokens: bfloat16 [32, 1184, 1024], P('replica', 'shard'), may hold values from -6 to 6
- image_count: int32 [32], P('replica'), may hold values from 1 to 2, as said below
- cotangent: bfloat16 [32, 1184, 1024], P('replica', 'shard'), may hold values from -6 to 6
- ln1_gain: bfloat16 [1024], P('shard'), may hold values from 0.5 to 1.5
- ln1_bias: bfloat16 [1024], P('shard'), may hold values from -1.75 to 1.75
- w_qkv: bfloat16 [1024, 3072], P('shard'), may hold values from -0.1875 to 0.1875
- b_query: bfloat16 [1024], P('shard'), may hold values from -1.75 to 1.75
- b_value: bfloat16 [1024], P('shard'), may hold values from -1.75 to 1.75
- w_out: bfloat16 [1024, 1024], P('shard'), may hold values from -1 to 1
- b_out: bfloat16 [1024], P('shard'), may hold values from -1.75 to 1.75
- ln2_gain: bfloat16 [1024], P('shard'), may hold values from 0.5 to 1.5
- ln2_bias: bfloat16 [1024], P('shard'), may hold values from -1.75 to 1.75
- w_fc1: bfloat16 [1024, 4096], P('shard'), may hold values from -0.1875 to 0.1875
- b_fc1: bfloat16 [4096], P('shard'), may hold values from -1.75 to 1.75
- w_fc2: bfloat16 [4096, 1024], P('shard'), may hold values from -0.125 to 0.125
- b_fc2: bfloat16 [1024], P('shard'), may hold values from -1.75 to 1.75
Outputs:
- out_tokens: bfloat16 [32, 1184, 1024], P('replica', 'shard')
- grad_tokens: float32 [32, 1184, 1024], P('replica', 'shard')
- grad_ln1_gain: float32 [1024], P('shard')
- grad_ln1_bias: float32 [1024], P('shard')
- grad_w_qkv: float32 [1024, 3072], P('shard')
- grad_b_query: float32 [1024], P('shard')
- grad_b_value: float32 [1024], P('shard')
- grad_w_out: float32 [1024, 1024], P('shard')
- grad_b_out: float32 [1024], P('shard')
- grad_ln2_gain: float32 [1024], P('shard')
- grad_ln2_bias: float32 [1024], P('shard')
- grad_w_fc1: float32 [1024, 4096], P('shard')
- grad_b_fc1: float32 [4096], P('shard')
- grad_w_fc2: float32 [4096, 1024], P('shard')
- grad_b_fc2: float32 [1024], P('shard')
Inputs may be any that keep to these rules, and one draw needn't show every extreme that they name: `image_count`: exactly 3 groups hold two images and the others one.
All inputs are finite; a program needn't handle non-finite values.
Results may differ from a plain program's by a relative error of at most 0.028.
Values may be sent and summed in bfloat16 or wider, within the bound.
No kernel may reach another device: no remote copies, remote signals or barrier semaphores. Data moves between devices by JAX's collectives and lax.ppermute only.
A program may use at most 192 MiB of HBM per device.

v0:
```python
import math

import jax
import jax.numpy as jnp
from jax import lax
from jax.sharding import PartitionSpec as P

HEAD_DIM = 64
IMG_LEN = 577


def sent_together(arrays, axis, dim, along):
    widths = [math.prod(a.shape[along:]) for a in arrays]
    both = jnp.concatenate(
        [a.reshape(*a.shape[:along], w) for a, w in zip(arrays, widths)], axis=along
    )
    filled = lax.psum_scatter(both, axis, scatter_dimension=dim, tiled=True)
    pieces = jnp.split(filled, [sum(widths[:k]) for k in range(1, len(widths))], axis=along)
    return tuple(
        (b.reshape(*filled.shape[:along], *a.shape[along:]) for a, b in zip(arrays, pieces))
    )


def norm(value, gain, shift):
    mean = jnp.mean(value, axis=-1, keepdims=True)
    centred = value - mean
    variance = jnp.mean(centred * centred, axis=-1, keepdims=True)
    return centred * lax.rsqrt(variance + 1e-06) * gain + shift


def blocked(matrix, rows):
    return matrix.reshape(rows, matrix.shape[1] // (2 * HEAD_DIM), 2, HEAD_DIM).transpose(
        1, 0, 2, 3
    )


def unblocked(blocks):
    return blocks.transpose(1, 0, 2, 3).reshape(blocks.shape[1], blocks.shape[0] * 2 * HEAD_DIM)


def body(
    tokens,
    image_count,
    cotangent,
    ln1_gain,
    ln1_bias,
    w_qkv,
    b_query,
    b_value,
    w_out,
    b_out,
    ln2_gain,
    ln2_bias,
    w_fc1,
    b_fc1,
    w_fc2,
    b_fc2,
):
    full = (
        lax.all_gather(ln1_gain, "shard", axis=0, tiled=True),
        lax.all_gather(ln1_bias, "shard", axis=0, tiled=True),
        lax.all_gather(w_qkv, "shard", axis=0, tiled=True),
        lax.all_gather(b_query, "shard", axis=0, tiled=True),
        lax.all_gather(b_value, "shard", axis=0, tiled=True),
        lax.all_gather(w_out, "shard", axis=0, tiled=True),
        lax.all_gather(b_out, "shard", axis=0, tiled=True),
        lax.all_gather(ln2_gain, "shard", axis=0, tiled=True),
        lax.all_gather(ln2_bias, "shard", axis=0, tiled=True),
        lax.all_gather(w_fc1, "shard", axis=0, tiled=True),
        lax.all_gather(b_fc1, "shard", axis=0, tiled=True),
        lax.all_gather(w_fc2, "shard", axis=0, tiled=True),
        lax.all_gather(b_fc2, "shard", axis=0, tiled=True),
    )
    (
        gain_one,
        shift_one,
        proj_qkv,
        bias_query,
        bias_value,
        proj_out,
        bias_out,
        gain_two,
        shift_two,
        proj_up,
        bias_up,
        proj_down,
        bias_down,
    ) = full
    rows_dev = tokens.shape[1]
    width = tokens.shape[2]
    group_rows = rows_dev * lax.axis_size("shard")
    local_rows = lax.axis_index("shard") * rows_dev + jnp.arange(rows_dev)
    key_rows = jnp.arange(group_rows)
    same = (local_rows // IMG_LEN)[:, None] == (key_rows // IMG_LEN)[None, :]
    valid = (local_rows < image_count[0] * IMG_LEN).astype(jnp.float32)
    value = tokens[0].astype(jnp.float32)
    gain_f1 = gain_one.astype(jnp.float32)
    shift_f1 = shift_one.astype(jnp.float32)
    gain_f2 = gain_two.astype(jnp.float32)
    shift_f2 = shift_two.astype(jnp.float32)
    first = norm(value, gain_f1, shift_f1).astype(jnp.bfloat16)
    packed = jnp.dot(first, proj_qkv, preferred_element_type=jnp.float32)
    query = (packed[:, :width] + bias_query.astype(jnp.float32)).astype(jnp.bfloat16)
    keys = packed[:, width : 2 * width].astype(jnp.bfloat16)
    values = (packed[:, 2 * width :] + bias_value.astype(jnp.float32)).astype(jnp.bfloat16)
    all_keys, all_values = (
        lax.all_gather(keys, "shard", axis=0, tiled=True),
        lax.all_gather(values, "shard", axis=0, tiled=True),
    )
    query_blocks = blocked(query, rows_dev)
    key_blocks = blocked(all_keys, group_rows)
    value_blocks = blocked(all_values, group_rows)

    def scores_of(query_block, key_block):
        scores = 0.125 * jnp.einsum(
            "rhd,shd->hrs", query_block, key_block, preferred_element_type=jnp.float32
        )
        return jnp.where(same[None], scores, -1e30)

    def attend_block(item):
        query_block, key_block, value_block = item
        scores = scores_of(query_block, key_block)
        peak = jnp.max(scores, axis=-1, keepdims=True)
        expo = jnp.exp(scores - peak)
        total = jnp.sum(expo, axis=-1, keepdims=True)
        weights = expo / total
        result = jnp.einsum(
            "hrs,shd->rhd",
            weights.astype(jnp.bfloat16),
            value_block,
            preferred_element_type=jnp.float32,
        )
        return (result, (peak + jnp.log(total))[..., 0])

    result_blocks, log_totals = lax.map(attend_block, (query_blocks, key_blocks, value_blocks))
    attended = unblocked(result_blocks).astype(jnp.bfloat16)
    middle = (
        value
        + jnp.dot(attended, proj_out, preferred_element_type=jnp.float32)
        + bias_out.astype(jnp.float32)
    )
    second = norm(middle, gain_f2, shift_f2).astype(jnp.bfloat16)
    hidden = jnp.dot(second, proj_up, preferred_element_type=jnp.float32) + bias_up.astype(
        jnp.float32
    )

    def gelu_exact(inner):
        return jax.nn.gelu(inner, approximate=False)

    act = gelu_exact(hidden).astype(jnp.bfloat16)
    result_tokens = (
        middle
        + jnp.dot(act, proj_down, preferred_element_type=jnp.float32)
        + bias_down.astype(jnp.float32)
    )
    out_tokens = result_tokens.astype(jnp.bfloat16)[None]
    (
        gain_one,
        shift_one,
        proj_qkv,
        bias_query,
        bias_value,
        proj_out,
        bias_out,
        gain_two,
        shift_two,
        proj_up,
        bias_up,
        proj_down,
        bias_down,
    ) = (
        lax.all_gather(ln1_gain, "shard", axis=0, tiled=True),
        lax.all_gather(ln1_bias, "shard", axis=0, tiled=True),
        lax.all_gather(w_qkv, "shard", axis=0, tiled=True),
        lax.all_gather(b_query, "shard", axis=0, tiled=True),
        lax.all_gather(b_value, "shard", axis=0, tiled=True),
        lax.all_gather(w_out, "shard", axis=0, tiled=True),
        lax.all_gather(b_out, "shard", axis=0, tiled=True),
        lax.all_gather(ln2_gain, "shard", axis=0, tiled=True),
        lax.all_gather(ln2_bias, "shard", axis=0, tiled=True),
        lax.all_gather(w_fc1, "shard", axis=0, tiled=True),
        lax.all_gather(b_fc1, "shard", axis=0, tiled=True),
        lax.all_gather(w_fc2, "shard", axis=0, tiled=True),
        lax.all_gather(b_fc2, "shard", axis=0, tiled=True),
    )
    d_out = cotangent[0].astype(jnp.float32) * valid[:, None]
    d_out_low = d_out.astype(jnp.bfloat16)
    grad_down = jnp.einsum("rf,rd->fd", act, d_out_low, preferred_element_type=jnp.float32)
    grad_bias_down = jnp.sum(d_out, axis=0)
    d_act = jnp.einsum("rd,fd->rf", d_out_low, proj_down, preferred_element_type=jnp.float32)
    gelu_value, gelu_pull = jax.vjp(gelu_exact, hidden)
    d_hidden = gelu_pull(d_act)[0].astype(jnp.bfloat16)
    grad_up = jnp.einsum("rd,rf->df", second, d_hidden, preferred_element_type=jnp.float32)
    grad_bias_up = jnp.sum(d_hidden.astype(jnp.float32), axis=0)
    d_second = jnp.einsum("rf,df->rd", d_hidden, proj_up, preferred_element_type=jnp.float32)
    norm_value, norm_pull = jax.vjp(norm, middle, gain_f2, shift_f2)
    d_middle_norm, grad_gain_two, grad_shift_two = norm_pull(d_second)
    d_middle = d_out + d_middle_norm
    d_branch = d_middle.astype(jnp.bfloat16)
    grad_out = jnp.einsum("rd,re->de", attended, d_branch, preferred_element_type=jnp.float32)
    grad_bias_out = jnp.sum(d_branch.astype(jnp.float32), axis=0)
    d_attended = jnp.einsum(
        "re,de->rd", d_branch, proj_out, preferred_element_type=jnp.float32
    ).astype(jnp.bfloat16)

    def attend_back(item):
        query_block, key_block, value_block, d_block, log_total = item
        weights = jnp.exp(scores_of(query_block, key_block) - log_total[..., None])
        d_weights = jnp.einsum(
            "rhd,shd->hrs", d_block, value_block, preferred_element_type=jnp.float32
        )
        d_scores = weights * (d_weights - jnp.sum(weights * d_weights, axis=-1, keepdims=True))
        d_scores = d_scores.astype(jnp.bfloat16)
        d_query_block = 0.125 * jnp.einsum(
            "hrs,shd->rhd", d_scores, key_block, preferred_element_type=jnp.float32
        )
        d_key_block = 0.125 * jnp.einsum(
            "hrs,rhd->shd", d_scores, query_block, preferred_element_type=jnp.float32
        )
        d_value_block = jnp.einsum(
            "hrs,rhd->shd",
            weights.astype(jnp.bfloat16),
            d_block,
            preferred_element_type=jnp.float32,
        )
        return (d_query_block, d_key_block, d_value_block)

    d_query_blocks, d_key_blocks, d_value_blocks = lax.map(
        attend_back,
        (query_blocks, key_blocks, value_blocks, blocked(d_attended, rows_dev), log_totals),
    )
    d_keys, d_values = (
        lax.psum_scatter(
            unblocked(d_key_blocks).astype(jnp.bfloat16), "shard", scatter_dimension=0, tiled=True
        ).astype(jnp.float32),
        lax.psum_scatter(
            unblocked(d_value_blocks).astype(jnp.bfloat16), "shard", scatter_dimension=0, tiled=True
        ).astype(jnp.float32),
    )
    d_query = unblocked(d_query_blocks).astype(jnp.bfloat16)
    d_keys = d_keys.astype(jnp.bfloat16)
    d_values = d_values.astype(jnp.bfloat16)
    d_packed = jnp.concatenate([d_query, d_keys, d_values], axis=1)
    grad_qkv = jnp.einsum("rd,re->de", first, d_packed, preferred_element_type=jnp.float32)
    grad_bias_query = jnp.sum(d_query.astype(jnp.float32), axis=0)
    grad_bias_value = jnp.sum(d_values.astype(jnp.float32), axis=0)
    d_first = jnp.einsum("re,de->rd", d_packed, proj_qkv, preferred_element_type=jnp.float32)
    first_value, first_pull = jax.vjp(norm, value, gain_f1, shift_f1)
    d_value_norm, grad_gain_one, grad_shift_one = first_pull(d_first)
    grad_tokens = (d_middle + d_value_norm)[None]
    owned = (
        lax.psum_scatter(
            grad_gain_one.astype(jnp.bfloat16), "shard", scatter_dimension=0, tiled=True
        ).astype(jnp.float32),
        *tuple(
            (
                part.astype(jnp.float32)
                for part in sent_together(
                    (
                        grad_shift_one.astype(jnp.bfloat16),
                        grad_qkv.astype(jnp.bfloat16),
                        grad_bias_query.astype(jnp.bfloat16),
                        grad_bias_value.astype(jnp.bfloat16),
                        grad_out.astype(jnp.bfloat16),
                        grad_bias_out.astype(jnp.bfloat16),
                        grad_gain_two.astype(jnp.bfloat16),
                        grad_shift_two.astype(jnp.bfloat16),
                        grad_up.astype(jnp.bfloat16),
                    ),
                    "shard",
                    0,
                    1,
                )
            )
        ),
        *tuple(
            (
                part.astype(jnp.float32)
                for part in sent_together(
                    (grad_bias_up.astype(jnp.bfloat16), grad_down.astype(jnp.bfloat16)),
                    "shard",
                    0,
                    1,
                )
            )
        ),
        lax.psum_scatter(
            grad_bias_down.astype(jnp.bfloat16), "shard", scatter_dimension=0, tiled=True
        ).astype(jnp.float32),
    )
    summed = (
        lax.psum(owned[0].astype(jnp.bfloat16), "replica").astype(jnp.float32),
        lax.psum(owned[1].astype(jnp.bfloat16), "replica").astype(jnp.float32),
        lax.psum(owned[2].astype(jnp.bfloat16), "replica").astype(jnp.float32),
        lax.psum(owned[3].astype(jnp.bfloat16), "replica").astype(jnp.float32),
        lax.psum(owned[4].astype(jnp.bfloat16), "replica").astype(jnp.float32),
        lax.psum(owned[5].astype(jnp.bfloat16), "replica").astype(jnp.float32),
        lax.psum(owned[6].astype(jnp.bfloat16), "replica").astype(jnp.float32),
        lax.psum(owned[7].astype(jnp.bfloat16), "replica").astype(jnp.float32),
        lax.psum(owned[8].astype(jnp.bfloat16), "replica").astype(jnp.float32),
        lax.psum(owned[9].astype(jnp.bfloat16), "replica").astype(jnp.float32),
        lax.psum(owned[10].astype(jnp.bfloat16), "replica").astype(jnp.float32),
        lax.psum(owned[11].astype(jnp.bfloat16), "replica").astype(jnp.float32),
        lax.psum(owned[12].astype(jnp.bfloat16), "replica").astype(jnp.float32),
    )
    return (
        out_tokens,
        grad_tokens,
        summed[0],
        summed[1],
        summed[2],
        summed[3],
        summed[4],
        summed[5],
        summed[6],
        summed[7],
        summed[8],
        summed[9],
        summed[10],
        summed[11],
        summed[12],
    )


def solution(mesh):
    in_specs = (
        P("replica", "shard", None),
        P("replica"),
        P("replica", "shard", None),
        P("shard"),
        P("shard"),
        P("shard", None),
        P("shard"),
        P("shard"),
        P("shard", None),
        P("shard"),
        P("shard"),
        P("shard"),
        P("shard", None),
        P("shard"),
        P("shard", None),
        P("shard"),
    )
    out_specs = (
        P("replica", "shard", None),
        P("replica", "shard", None),
        P("shard"),
        P("shard"),
        P("shard", None),
        P("shard"),
        P("shard"),
        P("shard", None),
        P("shard"),
        P("shard"),
        P("shard"),
        P("shard", None),
        P("shard"),
        P("shard", None),
        P("shard"),
    )
    return jax.shard_map(body, mesh=mesh, in_specs=in_specs, out_specs=out_specs, check_vma=False)
```

profile of v0, /device:TPU:0, one launch (start us, length us, event | category | flops | bytes accessed | tf_op | source)
XLA Modules:
  0.0 1168.5 jit_solution(8216561002355140092)
XLA Ops:
  33.1 42.2 %all-gather.15.cloned.1.call-done = bf16[1024,3072]{1,0:T(8,128)(2,1)} async-done(((bf16[256,3072]{1,0:T(8,128)(2,1)}), bf16[1024,3072]{1,0:T(8,128)(2,1)}) %all-gather.15.cloned.1.call-update) | async-done | bytes 6291472 | tf_op jit(solution)/shard_map/all_gather | solution.py:62
  102.8 5.4 all_gather.61
  110.0 6.9 all-gather.17.cloned.1.call-done
  121.2 30.6 %all-gather.19.cloned.1.call-done = bf16[1184,1024]{1,0:T(8,128)(2,1)} async-done(((bf16[296,1024]{1,0:T(8,128)(2,1)}), bf16[1184,1024]{1,0:T(8,128)(2,1)}) %all-gather.19.cloned.1.call-update) | async-done | bytes 2424848 | tf_op jit(solution)/shard_map/all_gather | solution.py:107
  155.8 40.8 %while.28 = (s32[]{:T(128)}, bf16[8,296,2,64]{1,3,2,0:T(8,128)(2,1)}, f32[8,2,296]{2,1,0:T(2,128)S(1)}, bf16[8,1184,2,64]{1,3,2,0:T(8,128)(2,1)}, bf16[8,296,2,6...) while((s32[]{:T(128)}, ...), condition=%wide.region_5.6_spmd.clone, body=%wide.region_2.5_spmd.clone.sunk | while | flops 185394864 | bytes 10119873 | solution.py:135
  201.1 65.1 %all-gather.23.cloned.1.call-done = bf16[1024,4096]{1,0:T(8,128)(2,1)} async-done(((bf16[256,4096]{1,0:T(8,128)(2,1)}), bf16[1024,4096]{1,0:T(8,128)(2,1)}) %all-gather.23.cloned.1.call-update) | async-done | bytes 8388624 | tf_op jit(solution)/shard_map/all_gather | solution.py:69
  266.2 18.3 %multiply_convert_fusion.1 = (bf16[296,4096]{1,0:T(8,128)(2,1)}, f32[296,4096]{1,0:T(8,128)}, f32[296,4096]{1,0:T(8,128)}) fusion(f32[4096]{0:T(1024)S(1)} %convert_element_type.274, bf16[1024,4096]{1,0:T(8,128)(2,1)} %all-gather.23.cloned.1.call-done, f32[296,1024]{1,0:T(8,128)} %copy-done.1, f32[1024]{0:T(1024)S(1)} %bitcast.228, f32[1024]{0:T(1024)S(1)} %bitcast.222, ...), kind=kOutput, calls=%fused_computation.65 | convolution fusion | flops 2564562944 | bytes 21752128 | tf_op jit(solution)/shard_map/dot_general | solution.py:143
  284.5 65.6 %all-gather.25.cloned.1.call-done = bf16[4096,1024]{1,0:T(8,128)(2,1)} async-done(((bf16[1024,1024]{1,0:T(8,128)(2,1)}), bf16[4096,1024]{1,0:T(8,128)(2,1)}) %all-gather.25.cloned.1.call-update) | async-done | bytes 8388624 | tf_op jit(solution)/shard_map/all_gather | solution.py:71
  350.1 10.8 fusion.102
  360.9 6.9 multiply_reduce_fusion.1
  376.0 78.8 %while.29 = (s32[]{:T(128)}, bf16[8,296,2,64]{1,3,2,0:T(8,128)(2,1)}, bf16[8,1184,2,64]{1,3,2,0:T(8,128)(2,1)}, bf16[8,1184,2,64]{1,3,2,0:T(8,128)(2,1)}, bf16[8...) while((s32[]{:T(128)}, ...), condition=%wide.region_12.13_spmd.clone, body=%wide.region_10.12_spmd.clone.sunk | while | flops 455441600 | bytes 25005464 | solution.py:228
  462.3 9.7 convolution_convert_fusion
  471.9 9.4 pad_maximum_fusion
  494.3 8.8 convolution_convert_fusion.1
  505.3 22.3 %reduce-scatter.15.cloned.1.call-done = bf16[296,1024]{1,0:T(8,128)(2,1)} async-done(((bf16[1184,1024]{1,0:T(8,128)(2,1)}), bf16[296,1024]{1,0:T(8,128)(2,1)}) %reduce-scatter.15.cloned.1.call-update) | async-done | bytes 606224
  529.8 6.8 fusion.95
  540.9 7.5 convolution_convert_fusion.2
  548.4 36.0 %concatenate.10 = bf16[1024,8198]{1,0:T(8,128)(2,1)} concatenate(bf16[1024,1]{1,0:T(8,128)(2,1)} %convert_element_type.331, bf16[1024,3072]{1,0:T(8,128)(2,1)} %convolution_convert_fusion.2, bf16[1024,1]{1,0:T(8,128)(2,1)S(1)} %reshape.283, bf16[1024,1]{1,0:T(8,128)(2,1)} %reshape.284, bf16[1024,1024]{1,0:T(8,128)(2,1)} %copy.56, bf16[1024,1]{1,0:T(8,128)(2,1)S(1)} %reshape.285, ...), dimensions={1} | concatenate | bytes 33579008 | tf_op jit(solution)/shard_map/concatenate | solution.py:14
  584.7 25.9 %reduce-scatter.11.cloned.1.call-done = bf16[1024,1025]{0,1:T(8,128)(2,1)} async-done(((bf16[4096,1025]{0,1:T(8,128)(2,1)}), bf16[1024,1025]{0,1:T(8,128)(2,1)}) %reduce-scatter.11.cloned.1.call-update) | async-done | bytes 2099216 | tf_op jit(solution)/shard_map/reduce_scatter | solution.py:17
  614.1 148.4 %reduce-scatter.9.cloned.1.call-done = bf16[256,8198]{1,0:T(8,128)(2,1)} async-done(((bf16[1024,8198]{1,0:T(8,128)(2,1)}), bf16[256,8198]{1,0:T(8,128)(2,1)}) %reduce-scatter.9.cloned.1.call-update) | async-done | bytes 4197392 | tf_op jit(solution)/shard_map/reduce_scatter | solution.py:17
  778.6 7.8 fusion.63
  789.3 6.4 all-reduce.4
  797.9 97.9 %all-reduce.2 = (bf16[256]{0:T(256)(128)(2,1)S(1)}, bf16[256]{0:T(256)(128)(2,1)S(1)}, bf16[256]{0:T(256)(128)(2,1)S(1)}, bf16[256]{0:T(256)(128)(2,1)S(1)}, bf1...) all-reduce(bf16[256]{0:T(256)(128)(2,1)S(1)} %dynamic-slice.1, ...), channel_id=1, replica_groups=mesh['shard'=4,'replica'=32] {'replica'}, use_global_device_ids=true, to_apply=%region_19.20 | all-reduce | flops 3072 | bytes 12288 | tf_op jit(solution)/shard_map/psum | solution.py:292
  901.0 248.9 %all-reduce.7.cloned.1.call-done = (bf16[1024,1024]{0,1:T(8,128)(2,1)}, bf16[256,3072]{1,0:T(8,128)(2,1)}, bf16[256,1024]{1,0:T(8,128)(2,1)}, bf16[256,4096]{1,0:T(8,128)(2,1)}) async-done(((bf16[1024,1024]{0,1:T(8,128)(2,1)}, bf16[256,3072]{1,0:T(8,128)(2,1)}, bf16[256,1024]{1,0:T(8,128)(2,1)}, bf16[256,4096]{1,0:T(8,128)(2,1)}), (bf16[1024,1024]{0,1:T(8,128)(2,1)}, bf16[256,3072]{1,0:T(8,128)(2,1)}, ...) | async-done | bytes 6291472 | tf_op jit(solution)/shard_map/psum | solution.py:303
  (316 shorter events, 264.4 us)
Async XLA Ops:
  7.2 25.0 %copy-start = (bf16[1,296,1024]{2,1,0:T(8,128)(2,1)S(1)}, bf16[1,296,1024]{2,1,0:T(8,128)(2,1)}, u32[]{:S(2)}) copy-start(bf16[1,296,1024]{2,1,0:T(8,128)(2,1)} %param.20) | copy-start | bytes 1818628
  7.2 68.1 %all-gather.15.cloned.1.call-start = ((), (), s32[]{:S(2)}) async-start(), calls=%async_computation.4 | async-start | bytes 7864320 | tf_op jit(solution)/shard_map/all_gather | solution.py:62
  7.9 109.0 %all-gather.17.cloned.1.call-start = ((), (), s32[]{:S(2)}) async-start(), calls=%async_computation.5 | async-start | bytes 3031040 | tf_op jit(solution)/shard_map/all_gather | solution.py:108
  13.7 66.6 %copy-start.15 = (f32[4,1,256]{2,1,0:T(1,128)}, f32[4,1,256]{2,1,0:T(1,128)S(1)}, u32[]{:S(2)}) copy-start(f32[4,1,256]{2,1,0:T(1,128)S(1)} %convert_element_type.320) | copy-start | bytes 12292
  19.4 60.9 %copy-start.34 = (f32[4,1,256]{2,1,0:T(1,128)}, f32[4,1,256]{2,1,0:T(1,128)S(1)}, u32[]{:S(2)}) copy-start(f32[4,1,256]{2,1,0:T(1,128)S(1)} %convert_element_type.321) | copy-start | bytes 12292
  32.1 48.2 %copy-start.17 = (f32[296]{0:T(512)}, f32[296]{0:T(512)S(1)}, u32[]{:S(2)}) copy-start(f32[296]{0:T(512)S(1)} %broadcast_multiply_fusion.1) | copy-start | bytes 3556
  33.1 47.2 %copy-start.23 = (f32[296]{0:T(512)}, f32[296]{0:T(512)S(1)}, u32[]{:S(2)}) copy-start(f32[296]{0:T(512)S(1)} %fusion.87) | copy-start | bytes 3556
  83.3 68.6 %all-gather.19.cloned.1.call-start = ((), (), s32[]{:S(2)}) async-start(), calls=%async_computation.6 | async-start | bytes 3031040 | tf_op jit(solution)/shard_map/all_gather | solution.py:107
  85.6 12.1 %copy-start.43 = (bf16[256]{0:T(256)(128)(2,1)S(1)}, bf16[256]{0:T(256)(128)(2,1)}, u32[]{:S(2)}) copy-start(bf16[256]{0:T(256)(128)(2,1)} %param.31) | copy-start | bytes 1540
  85.6 17.2 %copy-start.39 = (bf16[1024]{0:T(1024)(128)(2,1)S(1)}, bf16[1024]{0:T(1024)(128)(2,1)}, u32[]{:S(2)}) copy-start(bf16[1024]{0:T(1024)(128)(2,1)} %param.33) | copy-start | bytes 6148
  85.6 111.0 %all-gather.21.cloned.1.call-start = ((), (), s32[]{:S(2)}) async-start(), calls=%async_computation.7 | async-start | bytes 2621440 | tf_op jit(solution)/shard_map/all_gather | solution.py:65
  86.2 180.1 %all-gather.23.cloned.1.call-start = ((), (), s32[]{:S(2)}) async-start(), calls=%async_computation.8 | async-start | bytes 10485760 | tf_op jit(solution)/shard_map/all_gather | solution.py:69
  86.8 263.3 %all-gather.25.cloned.1.call-start = ((), (), s32[]{:S(2)}) async-start(), calls=%async_computation.9 | async-start | bytes 10485760 | tf_op jit(solution)/shard_map/all_gather | solution.py:71
  87.3 415.7 %reduce-scatter.13.cloned.1.call-start = ((), (), s32[]{:S(2)}) async-start(), calls=%async_computation.12 | async-start | bytes 3031040
  97.7 270.2 %copy-start.29 = (f32[4,1,256]{2,1,0:T(1,128)}, f32[4,1,256]{2,1,0:T(1,128)S(1)}, u32[]{:S(2)}) copy-start(f32[4,1,256]{2,1,0:T(1,128)S(1)} %convert_element_type.325) | copy-start | bytes 12292
  102.8 163.5 %copy-start.35 = (f32[4,1,256]{2,1,0:T(1,128)}, f32[4,1,256]{2,1,0:T(1,128)S(1)}, u32[]{:S(2)}) copy-start(f32[4,1,256]{2,1,0:T(1,128)S(1)} %convert_element_type.326) | copy-start | bytes 12292
  108.8 353.5 %copy-start.25 = (f32[296]{0:T(512)}, f32[296]{0:T(512)S(1)}, u32[]{:S(2)}) copy-start(f32[296]{0:T(512)S(1)} %fusion.86) | copy-start | bytes 3556
  199.8 168.0 %copy-start.19 = (f32[296]{0:T(512)}, f32[296]{0:T(512)S(1)}, u32[]{:S(2)}) copy-start(f32[296]{0:T(512)S(1)} %broadcast_multiply_fusion) | copy-start | bytes 3556
  201.1 166.7 %copy-start.31 = (f32[296]{0:T(512)}, f32[296]{0:T(512)S(1)}, u32[]{:S(2)}) copy-start(f32[296]{0:T(512)S(1)} %fusion.88) | copy-start | bytes 3556
  350.1 10.8 copy-start.2
  459.4 68.2 %reduce-scatter.15.cloned.1.call-start = ((), (), s32[]{:S(2)}) async-start(), calls=%async_computation.13 | async-start | bytes 3031040
  462.0 148.6 %reduce-scatter.11.cloned.1.call-start = ((), (), s32[]{:S(2)}) async-start(), calls=%async_computation.11 | async-start | bytes 10567680 | tf_op jit(solution)/shard_map/reduce_scatter | solution.py:17
  481.4 281.1 %reduce-scatter.9.cloned.1.call-start = ((), (), s32[]{:S(2)}) async-start(), calls=%async_computation.10 | async-start | bytes 21299200 | tf_op jit(solution)/shard_map/reduce_scatter | solution.py:17
  584.4 565.5 %all-reduce.7.cloned.1.call-start = ((), (), s32[]{:S(2)}) async-start(), calls=%async_computation.14 | async-start | bytes 12582912 | tf_op jit(solution)/shard_map/psum | solution.py:303
  (34 other events, 176.1 us)
Sparse Core Ops, SparseCore 0:
  9.7 65.5 all-gather.14
  83.4 33.4 all-gather.16
  119.1 32.6 all-gather.18
  153.4 30.0 all-gather.20
  185.0 81.2 all-gather.22
  267.8 82.2 all-gather.24
  459.5 32.9 reduce-scatter.12
  495.7 31.8 reduce-scatter.14
  530.0 80.5 reduce-scatter.10
  612.9 149.5 reduce-scatter.8
  771.7 378.1 all-reduce.6
where the time goes:
time: 1180 us; the launch traced here: 1170 us
  waiting for transfers between devices  658 us (56%)
  matrix products  197 us (17%)
  blocking collectives  150 us (13%)
  local copies, waits for them, and re-layouts  100 us (8%)
  other arithmetic  45.3 us (4%)
  between operations  16 us (1%)
    psum x1, waiting for transfers between devices, body(): lax.psum(owned[11].astype(jnp.bfloat16), 'replica').astype(jnp.float32)  249 us
    reduce_scatter x2, waiting for transfers between devices, sent_together(): filled = lax.psum_scatter(both, axis, scatter_dimension=dim, tiled=True)  174 us
    psum x1, blocking collectives, body(): lax.psum(owned[0].astype(jnp.bfloat16), 'replica').astype(jnp.float32)  97.9 us
    all_gather x1, waiting for transfers between devices, body(): lax.all_gather(w_fc2, 'shard', axis=0, tiled=True)  65.6 us
    all_gather x1, waiting for transfers between devices, body(): lax.all_gather(w_fc1, 'shard', axis=0, tiled=True)  65.1 us
    all_gather x1, waiting for transfers between devices, body(): lax.all_gather(w_qkv, 'shard', axis=0, tiled=True)  42.2 us
    concatenate x1, local copies, waits for them, and re-layouts, sent_together(): jnp.concatenate([a.reshape(*a.shape[:along], w) for a, w in zip(arrays, w...  36 us
    dot_general x16, matrix products, scores_of(): jnp.einsum('rhd,shd->hrs', query_block, key_block, preferred_element_type...  31.9 us
  transfers between devices with their start and end apart: 11, of which 9 were waited for; matrix products, arithmetic and copies ran while one was open for 17% of the time, Pallas kernels for 0%

commit v1 on v0

v1 whole, which is shorter than its diff:
```python
import jax
import jax.numpy as jnp
from jax import lax
from jax.experimental import pallas as pl
from jax.experimental.pallas import tpu as pltpu
from jax.sharding import PartitionSpec as P

HEAD_DIM = 64
IMG_LEN = 577
AXES = ("shard", "replica")
BF = jnp.bfloat16
F32 = jnp.float32
TAIL = 16


def place(index):
    shard, replica = divmod(index, 32)
    return (replica // 16) * 2 + shard // 2, (replica // 4) % 4, replica % 4, shard % 2


def index_of(y, z, x, core):
    y, z, x = y % 4, z % 4, x % 4
    return ((y % 2) * 2 + core) * 32 + (y // 2) * 16 + z * 4 + x


def moved(dy=0, dz=0, dx=0, dc=0):
    pairs = []
    for index in range(128):
        y, z, x, core = place(index)
        pairs.append((index, index_of(y + dy, z + dz, x + dx, (core + dc) % 2)))
    return pairs


CORE = moved(dc=1)
Y_UP = moved(dy=1)
Y_DOWN = moved(dy=-1)
Y_FAR = moved(dy=2)
X_BY = {d: moved(dx=d) for d in (1, 2, 3)}
Z_BY = {d: moved(dz=d) for d in (1, 2, 3)}
TO_FIRST = [(32 + r, 64 + r) for r in range(32)]
TO_SECOND = [(32 + r, 96 + r) for r in range(32)]
TAIL_BACK = [(96 + r, 32 + r) for r in range(32)]


def send(value, pairs):
    return lax.ppermute(value, AXES, pairs)


def dot(left, right, dims=((1,), (0,))):
    return lax.dot_general(left, right, (dims, ((), ())), preferred_element_type=F32)


def normed(value):
    mean = jnp.mean(value, axis=-1, keepdims=True)
    centred = value - mean
    variance = jnp.mean(centred * centred, axis=-1, keepdims=True)
    scale = lax.rsqrt(variance + 1e-06)
    return centred * scale, scale


def norm_back(d_value, unit, scale, gain):
    t = d_value * gain
    mean_t = jnp.mean(t, axis=-1, keepdims=True)
    mean_tn = jnp.mean(t * unit, axis=-1, keepdims=True)
    return scale * (t - mean_t - unit * mean_tn)


def attend_kernel(id_col, id_row, q_ref, k_ref, v_ref, out_ref, w_ref):
    q, k, v = q_ref[...], k_ref[...], v_ref[...]
    first_head = lax.broadcasted_iota(jnp.int32, q.shape, 1) < HEAD_DIM
    same = id_col[...] == id_row[...]
    zero = jnp.zeros_like(q)
    results = []
    for head in range(2):
        mine = first_head if head == 0 else jnp.logical_not(first_head)
        scores = 0.125 * dot(jnp.where(mine, q, zero), k, ((1,), (1,)))
        scores = jnp.where(same, scores, -1e30)
        peak = jnp.max(scores, axis=-1, keepdims=True)
        expo = jnp.exp(scores - peak)
        total = jnp.sum(expo, axis=-1, keepdims=True)
        weights = (expo * (1.0 / total)).astype(BF)
        w_ref[head] = weights
        results.append(dot(weights, v))
    out_ref[...] = jnp.where(first_head, results[0], results[1]).astype(BF)


def attend(ids, qkv):
    rows = qkv.shape[0]
    pairs = qkv.shape[1] // 3 // 128
    block = lambda off: pl.BlockSpec((rows, 128), lambda h: (0, h + off))
    return pl.pallas_call(
        attend_kernel,
        grid=(pairs,),
        in_specs=[
            pl.BlockSpec((rows, 1), lambda h: (0, 0)),
            pl.BlockSpec((1, rows), lambda h: (0, 0)),
            block(0),
            block(pairs),
            block(2 * pairs),
        ],
        out_specs=[block(0), pl.BlockSpec((2, rows, rows), lambda h: (h, 0, 0))],
        out_shape=[
            jax.ShapeDtypeStruct((rows, pairs * 128), BF),
            jax.ShapeDtypeStruct((2 * pairs, rows, rows), BF),
        ],
        compiler_params=pltpu.CompilerParams(vmem_limit_bytes=48 * 2**20),
        cost_estimate=pl.CostEstimate(
            flops=16 * pairs * rows * rows * 128, bytes_accessed=8 * 2**20, transcendentals=0
        ),
    )(ids[:, None], ids[None, :], qkv, qkv, qkv)


def attend_back_kernel(q_ref, k_ref, v_ref, d_ref, w_ref, dq_ref, dk_ref, dv_ref):
    q, k, v, d_out = q_ref[...], k_ref[...], v_ref[...], d_ref[...]
    first_head = lax.broadcasted_iota(jnp.int32, q.shape, 1) < HEAD_DIM
    zero = jnp.zeros_like(q)
    parts = []
    for head in range(2):
        mine = first_head if head == 0 else jnp.logical_not(first_head)
        low = w_ref[head]
        weights = low.astype(F32)
        d_weights = dot(jnp.where(mine, d_out, zero), v, ((1,), (1,)))
        both = weights * d_weights
        d_scores = (both - weights * jnp.sum(both, axis=-1, keepdims=True)).astype(BF)
        parts.append(
            (
                dot(d_scores, k),
                dot(d_scores, q, ((0,), (0,))),
                dot(low, d_out, ((0,), (0,))),
            )
        )
    dq_ref[...] = (0.125 * jnp.where(first_head, parts[0][0], parts[1][0])).astype(BF)
    dk_ref[...] = (0.125 * jnp.where(first_head, parts[0][1], parts[1][1])).astype(BF)
    dv_ref[...] = jnp.where(first_head, parts[0][2], parts[1][2]).astype(BF)


def attend_back(qkv, d_att, weights):
    rows = qkv.shape[0]
    pairs = qkv.shape[1] // 3 // 128
    block = lambda off: pl.BlockSpec((rows, 128), lambda h: (0, h + off))
    return pl.pallas_call(
        attend_back_kernel,
        grid=(pairs,),
        in_specs=[
            block(0),
            block(pairs),
            block(2 * pairs),
            block(0),
            pl.BlockSpec((2, rows, rows), lambda h: (h, 0, 0)),
        ],
        out_specs=[block(0)] * 3,
        out_shape=[jax.ShapeDtypeStruct((rows, pairs * 128), BF)] * 3,
        compiler_params=pltpu.CompilerParams(vmem_limit_bytes=48 * 2**20),
        cost_estimate=pl.CostEstimate(
            flops=32 * pairs * rows * rows * 128, bytes_accessed=10 * 2**20, transcendentals=0
        ),
    )(qkv, qkv, qkv, d_att, weights)


def body(
    tokens,
    image_count,
    cotangent,
    ln1_gain,
    ln1_bias,
    w_qkv,
    b_query,
    b_value,
    w_out,
    b_out,
    ln2_gain,
    ln2_bias,
    w_fc1,
    b_fc1,
    w_fc2,
    b_fc2,
):
    shard = lax.axis_index("shard")
    replica = lax.axis_index("replica")
    y_lo, core = shard // 2, shard % 2
    x_at, z_at = replica % 4, (replica // 4) % 4
    width = tokens.shape[2]
    rows_dev = tokens.shape[1]
    rows = 2 * rows_dev + TAIL
    mine = rows_dev + TAIL

    def ordered(flag, own, other, axis=0):
        return jnp.where(
            flag == 0,
            jnp.concatenate([own, other], axis),
            jnp.concatenate([other, own], axis),
        )

    def by_core(w, blocks, part):
        view = w.reshape(w.shape[0], blocks, 2, -1)
        return lax.dynamic_index_in_dim(view, part, 2, keepdims=False).reshape(w.shape[0], -1)

    def chip_half(w, blocks):
        kept = by_core(w, blocks, core)
        got = send(by_core(w, blocks, 1 - core), CORE)
        return jnp.where(core == 0, kept, got), jnp.where(core == 0, got, kept)

    def across(low, high):
        return send(low, Y_UP), send(high, Y_DOWN)

    small = jnp.stack(
        [ln1_gain, ln1_bias, b_query, b_value, b_out, ln2_gain, ln2_bias, b_fc2]
        + [b_fc1[256 * k : 256 * k + 256] for k in range(4)]
    )
    small = lax.all_gather(small, "shard", axis=0).astype(F32)
    vector = lambda k: small[:, k].reshape(-1)
    core_part = lambda v: lax.dynamic_index_in_dim(
        v.reshape(2, 2, -1), core, 1, keepdims=False
    ).reshape(-1)
    gain_1, shift_1, bias_out = vector(0), vector(1), vector(4)
    gain_2, shift_2, bias_down = vector(5), vector(6), vector(7)
    bias_query, bias_value = core_part(vector(2)), core_part(vector(3))
    bias_up = core_part(small[:, 8:12].reshape(-1))

    own = jnp.stack([tokens[0], cotangent[0]])
    other = send(own, CORE)
    tail = own[:, rows_dev - TAIL :]
    tail_low, tail_high = send(tail, TO_FIRST), send(tail, TO_SECOND)
    tail = jnp.where(core == 0, tail_low, tail_high)

    q_low, q_high = chip_half(w_qkv, 6)
    q_got = across(q_low, q_high)
    o_got = across(w_out[:128], w_out[128:])
    u_low, u_high = chip_half(w_fc1, 2)
    u_low, u_high, _ = lax.optimization_barrier((u_low, u_high, q_got))
    u_got = across(u_low, u_high)
    d_low, d_high, _ = lax.optimization_barrier((w_fc2[:512], w_fc2[512:], o_got))
    d_got = across(d_low, d_high)

    cat = lambda pair: jnp.concatenate(pair, 0)
    proj_qkv = ordered(y_lo, cat((q_low, q_high)), cat(q_got))
    proj_out = ordered(y_lo, w_out, cat(o_got))
    proj_up = ordered(y_lo, cat((u_low, u_high)), cat(u_got))
    proj_down = ordered(y_lo, cat((d_low, d_high)), cat(d_got))

    everything = jnp.concatenate([ordered(core, own, other, 1), tail], axis=1)
    at = jnp.arange(rows)
    chip_rows = 2 * rows_dev
    second_end = 2 * IMG_LEN - chip_rows
    ids_first = jnp.where(at < IMG_LEN, 0, 1)
    ids_second = jnp.where(
        (at < second_end) | (at > chip_rows), 0, jnp.where(at == chip_rows, 2, 1)
    )
    ids = jnp.where(y_lo == 0, ids_first, ids_second)
    valid = ((ids == 0) & (image_count[0] > y_lo)).astype(F32)

    value = everything[0].astype(F32)
    unit_1, scale_1 = normed(value)
    first = (unit_1 * gain_1 + shift_1).astype(BF)
    packed = dot(first, proj_qkv)
    qkv = (packed + jnp.concatenate([bias_query, jnp.zeros_like(bias_query), bias_value])).astype(
        BF
    )
    attended, weights = attend(ids, qkv)
    z_part = dot(attended, proj_out)
    middle = value + z_part + send(z_part.astype(BF), CORE).astype(F32) + bias_out
    unit_2, scale_2 = normed(middle)
    second = (unit_2 * gain_2 + shift_2).astype(BF)
    hidden = dot(second, proj_up) + bias_up
    cdf = 0.5 * (1.0 + lax.erf(hidden * (0.5**0.5)))
    act = (hidden * cdf).astype(BF)
    slope = (cdf + hidden * (0.3989422804014327 * jnp.exp(-0.5 * hidden * hidden))).astype(BF)

    pick = lambda v, who: lax.dynamic_slice_in_dim(v, who * rows_dev, mine, 0)
    y_part = dot(act, proj_down)
    y_got = send(pick(y_part, 1 - core).astype(BF), CORE)
    out = (pick(middle, core) + pick(y_part, core) + y_got.astype(F32) + bias_down).astype(BF)

    d_out = everything[1].astype(F32) * valid[:, None]
    d_low_out = d_out.astype(BF)
    grad_down = dot(act, d_low_out, ((0,), (0,))).astype(BF)
    d_act = dot(d_low_out, proj_down, ((1,), (1,)))
    d_hidden = (d_act * slope.astype(F32)).astype(BF)
    grad_up = dot(second, d_hidden, ((0,), (0,))).astype(BF)
    d_second = dot(d_hidden, proj_up, ((1,), (1,)))
    d_second = d_second + send(d_second.astype(BF), CORE).astype(F32)
    d_middle = d_out + norm_back(d_second, unit_2, scale_2, gain_2)
    d_branch = d_middle.astype(BF)
    grad_out = dot(attended, d_branch, ((0,), (0,))).astype(BF)
    d_attended = dot(d_branch, proj_out, ((1,), (1,))).astype(BF)
    d_qkv = jnp.concatenate(attend_back(qkv, d_attended, weights), axis=1)
    grad_qkv = dot(first, d_qkv, ((0,), (0,))).astype(BF)
    d_first = dot(d_qkv, proj_qkv, ((1,), (1,)))
    d_first_got = send(pick(d_first, 1 - core).astype(BF), CORE)
    d_first = pick(d_first, core) + d_first_got.astype(F32)
    unit_1, scale_1 = pick(unit_1, core), pick(scale_1, core)
    grad_tokens = pick(d_middle, core) + norm_back(d_first, unit_1, scale_1, gain_1)

    out_tail = send(out[rows_dev:], TAIL_BACK)
    grad_tail = send(grad_tokens[rows_dev:], TAIL_BACK)
    local = jnp.arange(rows_dev)[:, None] + rows_dev
    swapped = (shard == 1) & (local >= IMG_LEN)

    def with_tail(v, last):
        wide = jnp.concatenate([v[: rows_dev - TAIL], last], axis=0)
        return jnp.where(swapped, wide, v[:rows_dev])[None]

    out_tokens = with_tail(out, out_tail)
    grad_tokens = with_tail(grad_tokens, grad_tail)

    def ring_sum(v, at, by):
        step = v.shape[1] // 4
        chunk = lambda d: lax.dynamic_slice_in_dim(v, ((at + d) % 4) * step, step, 1)
        total = chunk(0).astype(F32)
        for d in (1, 3, 2):
            total = total + send(chunk(d), by[d]).astype(F32)
        return total.astype(BF)

    def ring_gather(v, at, by):
        pieces = [v] + [send(v, by[d]) for d in (1, 2, 3)]
        return jnp.concatenate(
            [lax.select_n((at - p) % 4, *pieces) for p in range(4)], axis=1
        )

    def chip_sum(grad, x_first, exchange):
        half = grad.shape[2] // 2
        kept = lax.dynamic_index_in_dim(grad, y_lo, 0, keepdims=False)
        given = lax.dynamic_index_in_dim(grad, 1 - y_lo, 0, keepdims=False)
        low = send(given[:, :half], Y_UP)
        high = send(given[:, half:], Y_DOWN)
        v = (kept.astype(F32) + jnp.concatenate([low, high], 1).astype(F32)).astype(BF)
        ways = [(x_at, X_BY), (z_at, Z_BY)]
        if not x_first:
            ways = ways[::-1]
        for way in ways:
            v = ring_sum(v, *way)
        v = (v.astype(F32) + send(v, Y_FAR).astype(F32)).astype(BF)
        if exchange:
            kept = lax.dynamic_index_in_dim(v, core, 0)
            got = send(lax.dynamic_index_in_dim(v, 1 - core, 0), CORE)
            v = ordered(core, kept, got, 0)
        for way in ways[::-1]:
            v = ring_gather(v, *way)
        return v.astype(F32)

    total_down = chip_sum(grad_down.reshape(2, 1, 1024, 1024), True, False)[0]
    total_up = chip_sum(grad_up.reshape(2, 2, 256, 2048), False, True)
    total_up = total_up.reshape(2, 256, 2, 1024).transpose(1, 2, 0, 3).reshape(256, 4096)
    total_out = chip_sum(grad_out.reshape(2, 1, 256, 1024), False, False)[0]
    total_qkv = chip_sum(grad_qkv.reshape(2, 2, 256, 1536), True, True)
    total_qkv = total_qkv.reshape(2, 256, 6, 256).transpose(1, 2, 0, 3).reshape(256, 3072)

    once = (core == 0).astype(F32)
    hot = (jnp.arange(2) == core).astype(F32)[None, :, None]
    spread = lambda v: (v.reshape(2, 1, -1) * hot).reshape(-1)
    kept_rows = (jnp.arange(mine) < rows_dev + TAIL * core).astype(F32)[:, None]
    d_first_kept = d_first * kept_rows
    over = lambda v: jnp.sum(v, axis=0)
    d_qkv_f = over(d_qkv.astype(F32))
    sums = jnp.concatenate(
        [
            over(d_first_kept * unit_1),
            over(d_first_kept),
            spread(d_qkv_f[:512]),
            spread(d_qkv_f[1024:]),
            once * over(d_branch.astype(F32)),
            once * over(d_second * unit_2),
            once * over(d_second),
            once * over(d_out),
            spread(over(d_hidden.astype(F32))),
        ]
    )
    sums = lax.psum(sums.reshape(12, 1024), AXES)
    vec = lambda k: lax.dynamic_slice_in_dim(sums[k], shard * 256, 256, 0)
    grad_up_bias = lax.dynamic_slice_in_dim(sums[8:].reshape(-1), shard * 1024, 1024, 0)
    return (
        out_tokens,
        grad_tokens,
        vec(0),
        vec(1),
        total_qkv,
        vec(2),
        vec(3),
        total_out,
        vec(4),
        vec(5),
        vec(6),
        total_up,
        grad_up_bias,
        total_down,
        vec(7),
    )


def solution(mesh):
    tokens, row, both = P("replica", "shard", None), P("shard"), P("shard", None)
    in_specs = (
        tokens, P("replica"), tokens, row, row, both, row, row, both, row, row, row, both, row,
        both, row,
    )
    out_specs = (
        tokens, tokens, row, row, both, row, row, both, row, row, row, both, row, both, row,
    )
    return jax.shard_map(body, mesh=mesh, in_specs=in_specs, out_specs=out_specs, check_vma=False)
```

time: 1180 us -> 540 us (0.46)
  waiting for transfers between devices: 658 us -> 100 us
  starting transfers between devices: 0.82 us -> 151 us
  matrix products: 197 us -> 51.2 us
  blocking collectives: 150 us -> 70.8 us
  local copies, waits for them, and re-layouts: 100 us -> 69.4 us
  Pallas kernels: 0 us -> 22.4 us
  other arithmetic: 45.3 us -> 64.8 us
  between operations: 16 us -> 3.2 us
    psum x1 -> x0, waiting for transfers between devices: 249 us -> none  [body(): lax.psum(owned[11].astype(jnp.bfloat16), 'replica').astype(jnp.float32)]
    all_gather x6 -> x0, waiting for transfers between devices: 210 us -> none  [the longest x1 65.6 us: body(): lax.all_gather(w_fc2, 'shard', axis=0, tiled=True)]
    reduce_scatter x2 -> x0, waiting for transfers between devices: 174 us -> none  [sent_together(): filled = lax.psum_scatter(both, axis, scatter_dimension=dim, tiled=True)]
    ppermute x0 -> x81, starting transfers between devices: none -> 151 us  [send(): return lax.ppermute(value, AXES, pairs)]
    dot_general x68 -> x12, matrix products: 197 us -> 51.2 us  [dot(): lax.dot_general(left, right, (dims, ((), ())), preferred_element_type=F32)]
    ppermute x0 -> x81, waiting for transfers between devices: none -> 100 us  [send(): return lax.ppermute(value, AXES, pairs)]
    all_gather x9 -> x1, blocking collectives: 45.9 us -> 5.19 us  [body(): small = lax.all_gather(small, 'shard', axis=0).astype(F32)]
    psum x1, blocking collectives: 97.9 us -> 65.6 us  [body(): sums = lax.psum(sums.reshape(12, 1024), AXES)]
  transfers between devices with their start and end apart: 11 -> 81, of which waited for: 9 -> 24; matrix products, arithmetic and copies ran while one was open for 17% -> 30% of each run, Pallas kernels for 0% -> 4%
where the time goes in v1:
time: 540 us; the launch traced here: 533 us
  starting transfers between devices  151 us (28%)
  waiting for transfers between devices  100 us (19%)
  blocking collectives  70.8 us (13%)
  local copies, waits for them, and re-layouts  69.4 us (13%)
  other arithmetic  64.8 us (12%)
  matrix products  51.2 us (9%)
  Pallas kernels  22.4 us (4%)
    ppermute x81, starting transfers between devices, send(): return lax.ppermute(value, AXES, pairs)  151 us
    ppermute x81, waiting for transfers between devices, send(): return lax.ppermute(value, AXES, pairs)  100 us
    psum x1, blocking collectives, body(): sums = lax.psum(sums.reshape(12, 1024), AXES)  65.6 us
    dot_general x12, matrix products, dot(): lax.dot_general(left, right, (dims, ((), ())), preferred_element_type=F32)  51.2 us
    unnamed x183, local copies, waits for them, and re-layouts  17.4 us
    pallas_call x1, Pallas kernels, attend_back(): pl.pallas_call(attend_back_kernel, grid=(pairs,), in_specs=[block(0), blo...  12.1 us
  transfers between devices with their start and end apart: 81, of which 24 were waited for; matrix products, arithmetic and copies ran while one was open for 30% of the time, Pallas kernels for 4%

profile of v1, /device:TPU:0, one launch (start us, length us, event | category | flops | bytes accessed | tf_op | source)
XLA Modules:
  0.0 533.2 jit_solution(3122655362766910853)
XLA Ops:
  18.0 5.2 all-gather.1
  42.7 13.7 %collective-permute-done.5 = bf16[256,1536]{0,1:T(8,128)(2,1)S(1)} collective-permute-done((bf16[256,1536]{0,1:T(8,128)(2,1)S(1)}, bf16[256,1536]{0,1:T(8,128)(2,1)S(1)}, u32[]{:S(2)}, u32[]{:S(2)}) %collective-permute-start.5) | collective-permute-done | bytes 786464 | tf_op jit(solution)/shard_map/ppermute | solution.py:46
  62.6 10.2 %shard_map.271 = (bf16[608,512]{1,0:T(8,128)(2,1)S(1)}, bf16[8,608,608]{2,1,0:T(8,128)(2,1)}) custom-call(s32[608,1]{1,0:T(8,128)S(1)} %select_select_fusion.8.id_col, s32[1,608]{1,0:T(1,128)S(1)} %broadcast_select_fusion.1.id_row, bf16[608,1536]{1,0:T(8,128)(2,1)S(1)} %add_convert_fusion.q_ref.k_ref.v_ref, ...), custom_call_target="tpu_custom_call" | custom-call | flops 3028287488 | bytes 8388608 | tf_op jit(solution)/shard_map/pallas_call | solution.py:91
  85.7 4.8 maximum_select_fusion
  90.5 4.7 fusion.42
  95.9 5.2 multiply_convert_fusion.1
  101.1 5.4 %collective-permute-done.12 = bf16[512,1024]{1,0:T(8,128)(2,1)S(1)} collective-permute-done((bf16[512,1024]{1,0:T(8,128)(2,1)}, bf16[512,1024]{1,0:T(8,128)(2,1)S(1)}, u32[]{:S(2)}, u32[]{:S(2)}) %collective-permute-start.12) | collective-permute-done | bytes 1048608 | tf_op jit(solution)/shard_map/ppermute | solution.py:46
  111.2 5.2 convolution_convert_fusion.1
  116.4 14.3 %convert_reduce_fusion = (f32[2048]{0:T(1024)S(1)}, bf16[608,2048]{1,0:T(8,128)(2,1)}) fusion(f32[608,2048]{1,0:T(8,128)} %get-tuple-element.188, f32[2048]{0:T(1024)S(1)} %bitcast.163, bf16[512,1024]{1,0:T(8,128)(2,1)} %copy-done.66, bf16[512,1024]{1,0:T(8,128)(2,1)S(1)} %copy-done.65, bf16[512,1024]{1,0:T(8,128)(2,1)S(1)} %copy-done.28, ...), kind=kOutput, calls=%fused_computation.6 | convolution fusion | flops 2606331904 | bytes 12929409 | tf_op jit(solution)/shard_map/dot_general | solution.py:50
  130.7 5.8 %convolution_convert_fusion.2 = bf16[1024,2048]{1,0:T(8,128)(2,1)S(1)} fusion(bf16[608,2048]{1,0:T(8,128)(2,1)} %get-tuple-element.192, f32[608,1024]{1,0:T(8,128)S(1)} %get-tuple-element.79, f32[1024]{0:T(1024)S(1)} %bitcast.167, f32[1024]{0:T(1024)S(1)} %bitcast.151, f32[608]{0:T(1024)S(1)} %add_rsqrt_fusion, f32[608]{0:T(1024)S(1)} %broadcast_multiply_fusion.2), kind=kOutput, calls=%fused_computation.20 | convolution fusion | flops 2555346944 | bytes 9188096 | tf_op jit(solution)/shard_map/dot_general | solution.py:50
  147.8 4.6 fusion.56
  152.4 34.8 %collective-permute-start.16 = (bf16[608,1024]{1,0:T(8,128)(2,1)}, bf16[608,1024]{1,0:T(8,128)(2,1)S(1)}, u32[]{:S(2)}, u32[]{:S(2)}) collective-permute-start(bf16[608,1024]{1,0:T(8,128)(2,1)} %get-tuple-element.189), channel_id=1, source_target_pairs={{0,32},{1,33},{2,34},{3,35},{4,36},{5,37},{6,38},{7,39},{8,40},{9,... | collective-permute-start | bytes 3735560 | tf_op jit(solution)/shard_map/ppermute | solution.py:46
  210.8 12.1 %shard_map.272 = (bf16[608,512]{1,0:T(8,128)(2,1)S(1)}, bf16[608,512]{1,0:T(8,128)(2,1)S(1)}, bf16[608,512]{1,0:T(8,128)(2,1)S(1)}) custom-call(bf16[608,1536]{1,0:T(8,128)(2,1)S(1)} %add_convert_fusion.q_ref.k_ref.v_ref, bf16[608,1536]{1,0:T(8,128)(2,1)S(1)} %add_convert_fusion.q_ref.k_ref.v_ref, bf16[608,1536]{1,0:T(8,128)(2,1)S(1)} %add_convert_fusion.q_ref.k_ref.v_ref, ...), custom_call_target="tpu_custom_call" | custom-call | flops 6056574976 | bytes 10485760 | tf_op jit(solution)/shard_map/pallas_call | solution.py:141
  251.0 5.6 %collective-permute-done.52 = bf16[2,64,2048]{2,1,0:T(8,128)(2,1)S(1)} collective-permute-done((bf16[2,64,2048]{2,1,0:T(8,128)(2,1)}, bf16[2,64,2048]{2,1,0:T(8,128)(2,1)S(1)}, u32[]{:S(2)}, u32[]{:S(2)}) %collective-permute-start.52) | collective-permute-done | bytes 524320 | tf_op jit(solution)/shard_map/ppermute | solution.py:46
  256.7 8.7 %collective-permute-start.37 = (bf16[1,64,1024]{2,1,0:T(8,128)(2,1)S(1)}, bf16[1,64,1024]{2,1,0:T(8,128)(2,1)S(1)}, u32[]{:S(2)}, u32[]{:S(2)}) collective-permute-start(bf16[1,64,1024]{2,1,0:T(8,128)(2,1)S(1)} %get-tuple-element.138), channel_id=1, source_target_pairs={{0,4},{1,5},{2,6},{3,7},{4,8},{5,9},{6,10},{7,11},{8,12},{9,13},{1... | collective-permute-start | bytes 393224 | tf_op jit(solution)/shard_map/ppermute | solution.py:46
  288.7 4.3 collective-permute-start.73
  330.8 65.6 %psum.7 = f32[12,1024]{1,0:T(8,128)} all-reduce(f32[12,1024]{1,0:T(8,128)S(1)} %reshape.469), channel_id=1, replica_groups=mesh['shard'=4,'replica'=32] {'shard','replica'}, use_global_device_ids=true, to_apply=%region_16.17 | all-reduce | flops 12288 | bytes 98304 | tf_op jit(solution)/shard_map/psum | solution.py:368
  427.6 15.2 %collective-permute-done.21 = bf16[2,64,1536]{2,1,0:T(8,128)(2,1)S(1)} collective-permute-done((bf16[2,64,1536]{2,1,0:T(8,128)(2,1)S(1)}, bf16[2,64,1536]{2,1,0:T(8,128)(2,1)S(1)}, u32[]{:S(2)}, u32[]{:S(2)}) %collective-permute-start.21) | collective-permute-done | bytes 393248 | tf_op jit(solution)/shard_map/ppermute | solution.py:46
  442.8 7.0 %collective-permute-done.23 = bf16[2,64,1536]{2,1,0:T(8,128)(2,1)S(1)} collective-permute-done((bf16[2,64,1536]{2,1,0:T(8,128)(2,1)S(1)}, bf16[2,64,1536]{2,1,0:T(8,128)(2,1)S(1)}, u32[]{:S(2)}, u32[]{:S(2)}) %collective-permute-start.23) | collective-permute-done | bytes 393248 | tf_op jit(solution)/shard_map/ppermute | solution.py:46
  451.5 9.1 %collective-permute-done.22 = bf16[2,64,1536]{2,1,0:T(8,128)(2,1)S(1)} collective-permute-done((bf16[2,64,1536]{2,1,0:T(8,128)(2,1)S(1)}, bf16[2,64,1536]{2,1,0:T(8,128)(2,1)S(1)}, u32[]{:S(2)}, u32[]{:S(2)}) %collective-permute-start.22) | collective-permute-done | bytes 393248 | tf_op jit(solution)/shard_map/ppermute | solution.py:46
  470.7 9.9 %collective-permute-done.25 = bf16[2,16,1536]{2,1,0:T(8,128)(2,1)S(1)} collective-permute-done((bf16[2,16,1536]{2,1,0:T(8,128)(2,1)S(1)}, bf16[2,16,1536]{2,1,0:T(8,128)(2,1)S(1)}, u32[]{:S(2)}, u32[]{:S(2)}) %collective-permute-start.25) | collective-permute-done | bytes 98336 | tf_op jit(solution)/shard_map/ppermute | solution.py:46
  500.0 4.8 collective-permute-start.34
  508.9 6.6 %reshape.486 = f32[256,4096]{1,0:T(8,128)} reshape(f32[256,2,2,1024]{3,2,1,0:T(2,128)} %convert_bitcast_fusion) | data formatting | bytes 8388608 | tf_op jit(solution)/shard_map/reshape | solution.py:343
  515.5 5.0 collective-permute-done.34
  (500 shorter events, 262.0 us)
Async XLA Ops:
  6.8 31.0 %collective-permute-start = (bf16[2,296,1024]{2,1,0:T(8,128)(2,1)}, bf16[2,296,1024]{2,1,0:T(8,128)(2,1)}, u32[]{:S(2)}, u32[]{:S(2)}) collective-permute-start(bf16[2,296,1024]{2,1,0:T(8,128)(2,1)} %constant_dynamic-update-slice_fusion), channel_id=1, source_target_pairs={{0,32},{1,33},{2,34},{3,35},{4,36},{5,37},{6,38},{7,39},{8,40},{9,... | collective-permute-start | bytes 3637256 | tf_op jit(solution)/shard_map/ppermute | solution.py:46
  30.0 42.9 %collective-permute-start.6 = (bf16[128,1024]{1,0:T(8,128)(2,1)}, bf16[128,1024]{1,0:T(8,128)(2,1)S(1)}, u32[]{:S(2)}, u32[]{:S(2)}) collective-permute-start(bf16[128,1024]{1,0:T(8,128)(2,1)} %get-tuple-element.143), channel_id=1, source_target_pairs={{0,64},{1,65},{2,66},{3,67},{4,68},{5,69},{6,70},{7,71},{8,72},{9,... | collective-permute-start | bytes 786440 | tf_op jit(solution)/shard_map/ppermute | solution.py:46
  30.0 42.8 %collective-permute-start.7 = (bf16[128,1024]{1,0:T(8,128)(2,1)}, bf16[128,1024]{1,0:T(8,128)(2,1)S(1)}, u32[]{:S(2)}, u32[]{:S(2)}) collective-permute-start(bf16[128,1024]{1,0:T(8,128)(2,1)} %get-tuple-element.144), channel_id=1, source_target_pairs={{0,80},{1,81},{2,82},{3,83},{4,84},{5,85},{6,86},{7,87},{8,88},{9,... | collective-permute-start | bytes 786440 | tf_op jit(solution)/shard_map/ppermute | solution.py:46
  56.8 28.9 %collective-permute-start.10 = (bf16[256,2048]{0,1:T(8,128)(2,1)}, bf16[256,2048]{0,1:T(8,128)(2,1)}, u32[]{:S(2)}, u32[]{:S(2)}) collective-permute-start(bf16[256,2048]{0,1:T(8,128)(2,1)} %get-tuple-element.25), channel_id=1, source_target_pairs={{0,64},{1,65},{2,66},{3,67},{4,68},{5,69},{6,70},{7,71},{8,72},{9,... | collective-permute-start | bytes 3145736 | tf_op jit(solution)/shard_map/ppermute | solution.py:46
  58.2 27.5 %collective-permute-start.11 = (bf16[256,2048]{0,1:T(8,128)(2,1)S(1)}, bf16[256,2048]{0,1:T(8,128)(2,1)}, u32[]{:S(2)}, u32[]{:S(2)}) collective-permute-start(bf16[256,2048]{0,1:T(8,128)(2,1)S(1)} %get-tuple-element.26), channel_id=1, source_target_pairs={{0,80},{1,81},{2,82},{3,83},{4,84},{5,85},{6,86},{7,87},{8,88},{9,... | collective-permute-start | bytes 3145736 | tf_op jit(solution)/shard_map/ppermute | solution.py:46
  110.6 36.1 %collective-permute-start.14 = (bf16[312,1024]{1,0:T(8,128)(2,1)S(1)}, bf16[312,1024]{1,0:T(8,128)(2,1)S(1)}, u32[]{:S(2)}, u32[]{:S(2)}) collective-permute-start(bf16[312,1024]{1,0:T(8,128)(2,1)S(1)} %dynamic-slice_convert_fusion.1), channel_id=1, source_target_pairs={{0,32},{1,33},{2,34},{3,35},{4,36},{5,37},{6,38},{7,39},{8,40},{9,... | collective-permute-start | bytes 1916936 | tf_op jit(solution)/shard_map/ppermute | solution.py:46
  138.5 49.9 %collective-permute-start.66 = (bf16[1,512,1024]{2,1,0:T(8,128)(2,1)}, bf16[1,512,1024]{2,1,0:T(8,128)(2,1)}, u32[]{:S(2)}, u32[]{:S(2)}) collective-permute-start(bf16[1,512,1024]{2,1,0:T(8,128)(2,1)} %get-tuple-element.89), channel_id=1, source_target_pairs={{0,64},{1,65},{2,66},{3,67},{4,68},{5,69},{6,70},{7,71},{8,72},{9,... | collective-permute-start | bytes 3145736 | tf_op jit(solution)/shard_map/ppermute | solution.py:46
  138.5 49.9 %collective-permute-start.67 = (bf16[1,512,1024]{2,1,0:T(8,128)(2,1)}, bf16[1,512,1024]{2,1,0:T(8,128)(2,1)}, u32[]{:S(2)}, u32[]{:S(2)}) collective-permute-start(bf16[1,512,1024]{2,1,0:T(8,128)(2,1)} %get-tuple-element.90), channel_id=1, source_target_pairs={{0,80},{1,81},{2,82},{3,83},{4,84},{5,85},{6,86},{7,87},{8,88},{9,... | collective-permute-start | bytes 3145736 | tf_op jit(solution)/shard_map/ppermute | solution.py:46
  143.5 53.8 %collective-permute-start.50 = (bf16[2,128,2048]{2,1,0:T(8,128)(2,1)}, bf16[2,128,2048]{2,1,0:T(8,128)(2,1)}, u32[]{:S(2)}, u32[]{:S(2)}) collective-permute-start(bf16[2,128,2048]{2,1,0:T(8,128)(2,1)} %get-tuple-element.98), channel_id=1, source_target_pairs={{0,64},{1,65},{2,66},{3,67},{4,68},{5,69},{6,70},{7,71},{8,72},{9,... | collective-permute-start | bytes 3145736 | tf_op jit(solution)/shard_map/ppermute | solution.py:46
  143.5 55.4 %collective-permute-start.51 = (bf16[2,128,2048]{2,1,0:T(8,128)(2,1)}, bf16[2,128,2048]{2,1,0:T(8,128)(2,1)}, u32[]{:S(2)}, u32[]{:S(2)}) collective-permute-start(bf16[2,128,2048]{2,1,0:T(8,128)(2,1)} %get-tuple-element.99), channel_id=1, source_target_pairs={{0,80},{1,81},{2,82},{3,83},{4,84},{5,85},{6,86},{7,87},{8,88},{9,... | collective-permute-start | bytes 3145736 | tf_op jit(solution)/shard_map/ppermute | solution.py:46
  152.4 50.2 %collective-permute-start.16 = (bf16[608,1024]{1,0:T(8,128)(2,1)}, bf16[608,1024]{1,0:T(8,128)(2,1)S(1)}, u32[]{:S(2)}, u32[]{:S(2)}) collective-permute-start(bf16[608,1024]{1,0:T(8,128)(2,1)} %get-tuple-element.189), channel_id=1, source_target_pairs={{0,32},{1,33},{2,34},{3,35},{4,36},{5,37},{6,38},{7,39},{8,40},{9,... | collective-permute-start | bytes 3735560 | tf_op jit(solution)/shard_map/ppermute | solution.py:46
  193.1 53.2 %collective-permute-start.68 = (bf16[1,256,1024]{2,1,0:T(8,128)(2,1)}, bf16[1,256,1024]{2,1,0:T(8,128)(2,1)}, u32[]{:S(2)}, u32[]{:S(2)}) collective-permute-start(bf16[1,256,1024]{2,1,0:T(8,128)(2,1)} %get-tuple-element.86), channel_id=1, source_target_pairs={{0,1},{1,2},{2,3},{3,0},{4,5},{5,6},{6,7},{7,4},{8,9},{9,10},{10,1... | collective-permute-start | bytes 1572872 | tf_op jit(solution)/shard_map/ppermute | solution.py:46
  194.5 53.9 %collective-permute-start.70 = (bf16[1,256,1024]{2,1,0:T(8,128)(2,1)}, bf16[1,256,1024]{2,1,0:T(8,128)(2,1)}, u32[]{:S(2)}, u32[]{:S(2)}) collective-permute-start(bf16[1,256,1024]{2,1,0:T(8,128)(2,1)} %get-tuple-element.87), channel_id=1, source_target_pairs={{0,2},{1,3},{2,0},{3,1},{4,6},{5,7},{6,4},{7,5},{8,10},{9,11},{10,... | collective-permute-start | bytes 1572872 | tf_op jit(solution)/shard_map/ppermute | solution.py:46
  197.3 51.3 %collective-permute-start.69 = (bf16[1,256,1024]{2,1,0:T(8,128)(2,1)}, bf16[1,256,1024]{2,1,0:T(8,128)(2,1)}, u32[]{:S(2)}, u32[]{:S(2)}) collective-permute-start(bf16[1,256,1024]{2,1,0:T(8,128)(2,1)} %get-tuple-element.88), channel_id=1, source_target_pairs={{0,3},{1,0},{2,1},{3,2},{4,7},{5,4},{6,5},{7,6},{8,11},{9,8},{10,9... | collective-permute-start | bytes 1572872 | tf_op jit(solution)/shard_map/ppermute | solution.py:46
  248.5 73.5 %collective-permute-start.17 = (bf16[312,1024]{1,0:T(8,128)(2,1)S(1)}, bf16[312,1024]{1,0:T(8,128)(2,1)S(1)}, u32[]{:S(2)}, u32[]{:S(2)}) collective-permute-start(bf16[312,1024]{1,0:T(8,128)(2,1)S(1)} %dynamic-slice_convert_fusion), channel_id=1, source_target_pairs={{0,32},{1,33},{2,34},{3,35},{4,36},{5,37},{6,38},{7,39},{8,40},{9,... | collective-permute-start | bytes 1916936 | tf_op jit(solution)/shard_map/ppermute | solution.py:46
  248.6 167.8 %collective-permute-start.19 = (bf16[2,128,1536]{2,1,0:T(8,128)(2,1)}, bf16[2,128,1536]{2,1,0:T(8,128)(2,1)S(1)}, u32[]{:S(2)}, u32[]{:S(2)}) collective-permute-start(bf16[2,128,1536]{2,1,0:T(8,128)(2,1)} %get-tuple-element.113), channel_id=1, source_target_pairs={{0,64},{1,65},{2,66},{3,67},{4,68},{5,69},{6,70},{7,71},{8,72},{9,... | collective-permute-start | bytes 2359304 | tf_op jit(solution)/shard_map/ppermute | solution.py:46
  315.9 103.2 %collective-permute-start.20 = (bf16[2,128,1536]{2,1,0:T(8,128)(2,1)}, bf16[2,128,1536]{2,1,0:T(8,128)(2,1)}, u32[]{:S(2)}, u32[]{:S(2)}) collective-permute-start(bf16[2,128,1536]{2,1,0:T(8,128)(2,1)} %get-tuple-element.114), channel_id=1, source_target_pairs={{0,80},{1,81},{2,82},{3,83},{4,84},{5,85},{6,86},{7,87},{8,88},{9,... | collective-permute-start | bytes 2359304 | tf_op jit(solution)/shard_map/ppermute | solution.py:46
  316.9 94.4 %collective-permute-start.77 = (bf16[1,64,1024]{2,1,0:T(8,128)(2,1)S(1)}, bf16[1,64,1024]{2,1,0:T(8,128)(2,1)}, u32[]{:S(2)}, u32[]{:S(2)}) collective-permute-start(bf16[1,64,1024]{2,1,0:T(8,128)(2,1)S(1)} %add_convert_fusion.9), channel_id=1, source_target_pairs={{0,12},{1,13},{2,14},{3,15},{4,0},{5,1},{6,2},{7,3},{8,4},{9,5},{1... | collective-permute-start | bytes 393224 | tf_op jit(solution)/shard_map/ppermute | solution.py:46
  320.6 91.7 %collective-permute-start.76 = (bf16[1,64,1024]{2,1,0:T(8,128)(2,1)S(1)}, bf16[1,64,1024]{2,1,0:T(8,128)(2,1)}, u32[]{:S(2)}, u32[]{:S(2)}) collective-permute-start(bf16[1,64,1024]{2,1,0:T(8,128)(2,1)S(1)} %add_convert_fusion.9), channel_id=1, source_target_pairs={{0,8},{1,9},{2,10},{3,11},{4,12},{5,13},{6,14},{7,15},{8,0},{9,1},... | collective-permute-start | bytes 393224 | tf_op jit(solution)/shard_map/ppermute | solution.py:46
  322.0 85.0 %collective-permute-start.59 = (bf16[1,16,2048]{2,1,0:T(8,128)(2,1)}, bf16[1,16,2048]{2,1,0:T(8,128)(2,1)}, u32[]{:S(2)}, u32[]{:S(2)}) collective-permute-start(bf16[1,16,2048]{2,1,0:T(8,128)(2,1)} %get-tuple-element.153), channel_id=1, source_target_pairs={{0,32},{1,33},{2,34},{3,35},{4,36},{5,37},{6,38},{7,39},{8,40},{9,... | collective-permute-start | bytes 196616 | tf_op jit(solution)/shard_map/ppermute | solution.py:46
  416.4 45.9 %collective-permute-start.79 = (bf16[1,256,1024]{2,1,0:T(8,128)(2,1)S(1)}, bf16[1,256,1024]{2,1,0:T(8,128)(2,1)S(1)}, u32[]{:S(2)}, u32[]{:S(2)}) collective-permute-start(bf16[1,256,1024]{2,1,0:T(8,128)(2,1)S(1)} %pad_maximum_fusion.2), channel_id=1, source_target_pairs={{0,2},{1,3},{2,0},{3,1},{4,6},{5,7},{6,4},{7,5},{8,10},{9,11},{10,... | collective-permute-start | bytes 1572872 | tf_op jit(solution)/shard_map/ppermute | solution.py:46
  419.1 43.9 %collective-permute-start.80 = (bf16[1,256,1024]{2,1,0:T(8,128)(2,1)S(1)}, bf16[1,256,1024]{2,1,0:T(8,128)(2,1)S(1)}, u32[]{:S(2)}, u32[]{:S(2)}) collective-permute-start(bf16[1,256,1024]{2,1,0:T(8,128)(2,1)S(1)} %pad_maximum_fusion.2), channel_id=1, source_target_pairs={{0,3},{1,0},{2,1},{3,2},{4,7},{5,4},{6,5},{7,6},{8,11},{9,8},{10,9... | collective-permute-start | bytes 1572872 | tf_op jit(solution)/shard_map/ppermute | solution.py:46
  424.0 36.6 %collective-permute-start.22 = (bf16[2,64,1536]{2,1,0:T(8,128)(2,1)S(1)}, bf16[2,64,1536]{2,1,0:T(8,128)(2,1)S(1)}, u32[]{:S(2)}, u32[]{:S(2)}) collective-permute-start(bf16[2,64,1536]{2,1,0:T(8,128)(2,1)S(1)} %get-tuple-element.112), channel_id=1, source_target_pairs={{0,3},{1,0},{2,1},{3,2},{4,7},{5,4},{6,5},{7,6},{8,11},{9,8},{10,9... | collective-permute-start | bytes 1179656 | tf_op jit(solution)/shard_map/ppermute | solution.py:46
  449.8 37.3 %collective-permute-start.64 = (bf16[2,64,2048]{2,1,0:T(8,128)(2,1)S(1)}, bf16[2,64,2048]{2,1,0:T(8,128)(2,1)S(1)}, u32[]{:S(2)}, u32[]{:S(2)}) collective-permute-start(bf16[2,64,2048]{2,1,0:T(8,128)(2,1)S(1)} %pad_maximum_fusion.1), channel_id=1, source_target_pairs={{0,8},{1,9},{2,10},{3,11},{4,12},{5,13},{6,14},{7,15},{8,0},{9,1},... | collective-permute-start | bytes 1572872 | tf_op jit(solution)/shard_map/ppermute | solution.py:46
  (141 other events, 1739.8 us)
